TPU v7x, 32 devices: a whole 2x2x4 slice. The times are simulated.
32 devices in a mesh: dp: 8 (over y, x, core), seq: 4 (over z).
Axes of the slice: x: 2, y: 2, z: 4, core: 2. Of those that a mesh axis runs over, the one named last changes fastest.
Arguments:
- enc_hidden: bfloat16 [8, 256, 5120], P('dp', None, 'seq'), may hold values from -6 to 6
- enc_wo: bfloat16 [5120, 4096], P('seq'), may hold values from -0.078125 to 0.078125
- enc_gain: float32 [4096], replicated, may hold values from 0.25 to 1.75
- text_len: int32 [8], P('dp'), may hold values from 1 to 256, as said below
- text_kv: bfloat16 [4096, 2, 2048], P(None, None, 'seq'), may hold values from -0.09375 to 0.09375
- lat_qkv: bfloat16 [8, 1024, 3, 2048], P('dp', 'seq')
- output_weight: bfloat16 [2048, 3072], P('seq'), may hold values from -0.125 to 0.125
- output_cotangent: bfloat16 [8, 1024, 3072], P('dp', 'seq'), may hold values from -6 to 6
Outputs:
- latent_block_output: bfloat16 [8, 1024, 3072], P('dp', 'seq')
- output_weight_gradient: float32 [2048, 3072], P('seq', 'dp')
Inputs may be any that keep to these rules, and one draw needn't show every extreme that they name: `text_len`: some sample has all 256 text tokens.
All inputs are finite; a program needn't handle non-finite values.
Results may differ from a plain program's by a relative error of at most 0.018.
Values may be sent and summed in bfloat16 or wider, within the bound.
A program may use at most 128 MiB of HBM per device.

v0:
```python
import jax
import jax.numpy as jnp
from jax import lax
from jax.sharding import PartitionSpec as P

HD = 128


def encoder_text(enc_hidden, enc_wo, enc_gain):
    partial_value = jnp.einsum(
        "ste,ed->std", enc_hidden, enc_wo, preferred_element_type=jnp.float32
    ).astype(jnp.bfloat16)
    summed = lax.psum(partial_value, "seq").astype(jnp.float32)
    meansq = jnp.mean(summed * summed, -1, keepdims=True)
    return (summed * lax.rsqrt(meansq + 1e-06) * enc_gain).astype(jnp.bfloat16)


def attend(gathered, text_pairs, text_len):
    samples, latent, _, local_width = gathered.shape
    heads_here = local_width // HD
    text_count = text_pairs.shape[1]
    keys = jnp.concatenate([gathered[:, :, 1], text_pairs[:, :, 0]], 1)
    keys = keys.reshape(samples, latent + text_count, heads_here, HD)
    values = jnp.concatenate([gathered[:, :, 2], text_pairs[:, :, 1]], 1)
    values = values.reshape(samples, latent + text_count, heads_here, HD)
    keep = jnp.concatenate(
        [jnp.ones((samples, latent), bool), jnp.arange(text_count)[None, :] < text_len[:, None]], 1
    )
    block_rows = min(512, latent)
    queries = gathered[:, :, 0].reshape(samples, latent // block_rows, block_rows, heads_here, HD)
    queries = jnp.moveaxis(queries, 1, 0)

    def one_block(query_block):
        scores = jnp.einsum(
            "sqhd,skhd->shqk", query_block, keys, preferred_element_type=jnp.float32
        ) * HD ** (-0.5)
        scores = jnp.where(keep[:, None, None, :], scores, -1e30)
        top = jnp.max(scores, -1, keepdims=True)
        weights = jnp.exp(scores - top)
        probs = (weights / jnp.sum(weights, -1, keepdims=True)).astype(jnp.bfloat16)
        result = jnp.einsum("shqk,skhd->sqhd", probs, values, preferred_element_type=jnp.float32)
        return result.reshape(samples, block_rows, local_width).astype(jnp.bfloat16)

    block_count = lax.map(one_block, queries)
    return jnp.moveaxis(block_count, 0, 1).reshape(samples, latent, local_width)


def shards(
    enc_hidden, enc_wo, enc_gain, text_len, text_kv, lat_qkv, output_weight, output_cotangent
):
    text_emb = encoder_text(enc_hidden, enc_wo, enc_gain)
    text_pairs = jnp.einsum(
        "std,dkh->stkh", text_emb, text_kv, preferred_element_type=jnp.float32
    ).astype(jnp.bfloat16)
    gathered = lax.all_to_all(lat_qkv, "seq", split_axis=3, concat_axis=1, tiled=True)
    attn_heads = attend(gathered, text_pairs, text_len)
    attention_token_rows = lax.all_to_all(
        attn_heads, "seq", split_axis=1, concat_axis=2, tiled=True
    )
    columns = attention_token_rows
    projected = jnp.einsum(
        "ugj,jn->ugn",
        columns,
        lax.all_gather(output_weight, "seq", axis=0, tiled=True),
        preferred_element_type=jnp.float32,
    )
    latent_block_output = projected.astype(jnp.bfloat16)
    partial_value = jnp.einsum(
        "vwk,vwy->ky", attention_token_rows, output_cotangent, preferred_element_type=jnp.float32
    )
    columns = lax.psum_scatter(
        partial_value.astype(jnp.bfloat16), "dp", scatter_dimension=1, tiled=True
    ).astype(jnp.float32)
    output_weight_gradient = lax.psum_scatter(
        columns.astype(jnp.bfloat16), "seq", scatter_dimension=0, tiled=True
    ).astype(jnp.float32)
    return (latent_block_output, output_weight_gradient)


def solution(mesh):
    placed = (
        P("dp", None, "seq"),
        P("seq", None),
        P(),
        P("dp"),
        P(None, None, "seq"),
        P("dp", "seq", None, None),
        P("seq", None),
        P("dp", "seq", None),
    )
    return jax.shard_map(
        shards,
        mesh=mesh,
        in_specs=placed,
        out_specs=(P("dp", "seq", None), P("seq", "dp")),
        check_vma=False,
    )
```

profile of v0, /device:TPU:0, one launch (start us, length us, event | category | flops | bytes accessed | tf_op | source)
XLA Modules:
  0.0 669.0 jit_solution(6397270061237196105)
XLA Ops:
  7.2 7.3 %copy.33 = bf16[1,256,3,2048]{1,2,0,3:T(4,128)(2,1)} copy(bf16[1,256,3,2048]{3,1,2,0:T(8,128)(2,1)} %param.15) | data formatting | bytes 6291456 | tf_op args[5]
  14.5 6.4 all-to-all-start
  20.9 8.0 %fusion.47 = bf16[1,256,4096]{2,1,0:T(8,128)(2,1)} fusion(bf16[1280,4096]{1,0:T(8,128)(2,1)} %param.11, bf16[1,256,1280]{2,1,0:T(8,128)(2,1)S(1)} %copy-done.1), kind=kOutput, calls=%fused_computation.34 | convolution fusion | flops 2685403136 | bytes 13238272 | tf_op jit(solution)/shard_map/ste,ed->std/dot_general | solution.py:10
  29.7 152.5 %all-reduce.3.cloned.1.call-done = bf16[1,256,4096]{2,1,0:T(8,128)(2,1)} async-done(((bf16[1,256,4096]{2,1,0:T(8,128)(2,1)}), bf16[1,256,4096]{2,1,0:T(8,128)(2,1)}) %all-reduce.3.cloned.1.call-update) | async-done | bytes 2097168 | tf_op jit(solution)/shard_map/psum | solution.py:13
  184.3 6.4 fusion.62
  191.1 6.8 %copy.61 = bf16[1,256,3,4,512]{1,3,4,2,0:T(4,128)(2,1)} copy(bf16[1,256,3,4,512]{1,2,4,3,0:T(4,128)(2,1)} %bitcast.8) | data formatting | bytes 6291456 | tf_op jit(solution)/shard_map/all_to_all | solution.py:55
  197.9 6.1 all_to_all.27
  204.0 3.6 fusion.73
  215.4 24.5 %while.10 = (s32[]{:T(128)}, bf16[2,1,512,512]{3,2,0,1:T(8,128)(2,1)}, pred[1,1280]{1,0:T(4,128)(4,1)S(1)}, bf16[2,1,512,4,128]{4,2,3,1,0:T(8,128)(2,1)}, bf16[1...) while((s32[]{:T(128)}, bf16[2,1,512,512]{3,2,0,1:T(8,128)(2,1)}, ...), condition=%wide.region_5.6_spmd, body=%wide.region_2.5_spmd.sunk | while | flops 2037125632 | bytes 7625302 | solution.py:44
  215.4 4.7 fusion.91
  220.1 6.4 fusion.92
  227.6 4.7 fusion.91
  232.3 6.4 fusion.92
  239.9 4.2 copy.62
  244.6 8.0 %reduce.6 = bf16[1024,512]{1,0:T(8,128)(2,1)S(1)} reduce(bf16[1024,1,512]{2,1,0:T(2,128)(2,1)} %bitcast.107, bf16[]{:T(256)} %broadcast.50), dimensions={1}, to_apply=%bitcast.87.reduce_sub_computation | reduce | bytes 2097154
  254.6 29.7 %all_to_all.33 = bf16[4,2,65536]{2,1,0:T(2,128)(2,1)S(1)} all-to-all(bf16[4,2,65536]{2,1,0:T(2,128)(2,1)} %reshape.120), channel_id=1, replica_groups=mesh['dp'=8,'seq'=4] {'seq'}, dimensions={0} | all-to-all | bytes 2097152 | tf_op jit(solution)/shard_map/all_to_all | solution.py:57
  286.6 2.8 copy.52
  291.0 6.5 convolution_convert_fusion
  297.4 15.7 %copy.48 = bf16[2048,3072]{0,1:T(8,128)(2,1)} copy(bf16[2048,3072]{1,0:T(8,128)(2,1)} %convolution_convert_fusion) | data formatting | bytes 25165824
  314.0 90.9 %reduce-scatter.7.cloned.1.call-done = bf16[384,2048]{1,0:T(8,128)(2,1)} async-done(((bf16[3072,2048]{1,0:T(8,128)(2,1)}), bf16[384,2048]{1,0:T(8,128)(2,1)}) %reduce-scatter.7.cloned.1.call-update) | async-done | bytes 1572880
  404.9 2.6 copy.49
  407.5 217.2 %all-gather.2.cloned.1.call-done = bf16[2048,3072]{1,0:T(8,128)(2,1)} async-done(((bf16[512,3072]{1,0:T(8,128)(2,1)}), bf16[2048,3072]{1,0:T(8,128)(2,1)}) %all-gather.2.cloned.1.call-update) | async-done | bytes 12582928 | tf_op jit(solution)/shard_map/all_gather | solution.py:64
  624.8 9.1 %fusion.51 = bf16[1,256,3072]{2,1,0:T(8,128)(2,1)} fusion(bf16[256,2048]{0,1:T(8,128)(2,1)S(1)} %bitcast.104, bf16[2048,3072]{1,0:T(8,128)(2,1)} %all-gather.2.cloned.1.call-done), kind=kOutput, calls=%fused_computation.39 | convolution fusion | flops 3222011904 | bytes 15204352 | tf_op jit(solution)/shard_map/ugj,jn->ugn/dot_general | solution.py:61
  633.9 26.6 %reduce-scatter.5.cloned.1.call-done = bf16[512,384]{1,0:T(8,128)(2,1)} async-done(((bf16[2048,384]{1,0:T(8,128)(2,1)}), bf16[512,384]{1,0:T(8,128)(2,1)}) %reduce-scatter.5.cloned.1.call-update) | async-done | bytes 393232 | tf_op jit(solution)/shard_map/reduce_scatter | solution.py:74
  (39 shorter events, 21.5 us)
Async XLA Ops:
  7.2 283.8 %copy-start = (bf16[1,256,3072]{2,1,0:T(8,128)(2,1)S(1)}, bf16[1,256,3072]{2,1,0:T(8,128)(2,1)}, u32[]{:S(2)}) copy-start(bf16[1,256,3072]{2,1,0:T(8,128)(2,1)} %param.17) | copy-start | bytes 4718596
  14.5 6.5 copy-start.1
  14.5 176.6 %all-to-all-start = ((bf16[1,256,3,2048]{1,2,0,3:T(4,128)(2,1)}), bf16[1,256,3,2048]{1,2,0,3:T(4,128)(2,1)}, u32[]{:S(2)}, u32[]{:S(2)}) async-start(bf16[1,256,3,2048]{1,2,0,3:T(4,128)(2,1)} %copy.33), calls=%async_computation | async-start | bytes 8388608 | tf_op jit(solution)/shard_map/all_to_all | solution.py:55
  20.9 161.3 %all-reduce.3.cloned.1.call-start = ((), (), s32[]{:S(2)}) async-start(), calls=%async_computation.4 | async-start | bytes 4194304 | tf_op jit(solution)/shard_map/psum | solution.py:13
  29.0 155.4 %copy-start.2 = (f32[4096]{0:T(1024)S(1)}, f32[4096]{0:T(1024)}, u32[]{:S(2)}) copy-start(f32[4096]{0:T(1024)} %param.12) | copy-start | bytes 49156
  29.0 375.9 %reduce-scatter.7.cloned.1.call-start = ((), (), s32[]{:S(2)}) async-start(), calls=%async_computation.7 | async-start | bytes 14155776
  313.2 311.6 %all-gather.2.cloned.1.call-start = ((), (), s32[]{:S(2)}) async-start(), calls=%async_computation.5 | async-start | bytes 15728640 | tf_op jit(solution)/shard_map/all_gather | solution.py:64
  313.9 346.6 %reduce-scatter.5.cloned.1.call-start = ((), (), s32[]{:S(2)}) async-start(), calls=%async_computation.6 | async-start | bytes 1966080 | tf_op jit(solution)/shard_map/reduce_scatter | solution.py:74
Sparse Core Ops, SparseCore 0:
  29.1 153.0 all-reduce.2
  313.3 91.5 reduce-scatter.6
  406.6 218.1 all-gather.1
  627.0 33.4 reduce-scatter.4
where the time goes:
time: 670 us; the launch traced here: 669 us
  waiting for transfers between devices  488 us (73%)
  local copies, waits for them, and re-layouts  63.3 us (9%)
  matrix products  52.3 us (8%)
  blocking collectives  29.7 us (4%)
  other arithmetic  14.6 us (2%)
  between operations  14.5 us (2%)
    all_gather x1, waiting for transfers between devices, shards(): lax.all_gather(output_weight, 'seq', axis=0, tiled=True)  217 us
    psum x1, waiting for transfers between devices, encoder_text(): summed = lax.psum(partial_value, 'seq').astype(jnp.float32)  153 us
    unnamed x5, waiting for transfers between devices  91.6 us
    unnamed x13, local copies, waits for them, and re-layouts  33.3 us
    all_to_all x1, blocking collectives, shards(): lax.all_to_all(attn_heads, 'seq', split_axis=1, concat_axis=2, tiled=True)  29.7 us
    reduce_scatter x1, waiting for transfers between devices, shards(): lax.psum_scatter(columns.astype(jnp.bfloat16), 'seq', scatter_dimension=0...  26.6 us
  transfers between devices with their start and end apart: 5, of which 4 were waited for; matrix products, arithmetic and copies ran while one was open for 4% of the time, Pallas kernels for 0%

commit v1 on v0

--- a/solution.py
+++ b/solution.py
@@ -49,6 +49,10 @@
     enc_hidden, enc_wo, enc_gain, text_len, text_kv, lat_qkv, output_weight, output_cotangent
 ):
     text_emb = encoder_text(enc_hidden, enc_wo, enc_gain)
+    share = output_weight.shape[0] // lax.axis_size("dp")
+    rows = lax.dynamic_slice_in_dim(output_weight, lax.axis_index("dp") * share, share, 0)
+    rows, text_emb = lax.optimization_barrier((rows, text_emb))
+    weight = lax.all_gather(rows, ("seq", "dp"), axis=0, tiled=True)
     text_pairs = jnp.einsum(
         "std,dkh->stkh", text_emb, text_kv, preferred_element_type=jnp.float32
     ).astype(jnp.bfloat16)
@@ -57,22 +61,23 @@
     attention_token_rows = lax.all_to_all(
         attn_heads, "seq", split_axis=1, concat_axis=2, tiled=True
     )
+    attention_token_rows, weight = lax.optimization_barrier((attention_token_rows, weight))
     columns = attention_token_rows
     projected = jnp.einsum(
         "ugj,jn->ugn",
         columns,
-        lax.all_gather(output_weight, "seq", axis=0, tiled=True),
+        weight,
         preferred_element_type=jnp.float32,
     )
     latent_block_output = projected.astype(jnp.bfloat16)
     partial_value = jnp.einsum(
-        "vwk,vwy->ky", attention_token_rows, output_cotangent, preferred_element_type=jnp.float32
+        "vwk,vwy->yk", attention_token_rows, output_cotangent, preferred_element_type=jnp.float32
     )
     columns = lax.psum_scatter(
-        partial_value.astype(jnp.bfloat16), "dp", scatter_dimension=1, tiled=True
-    ).astype(jnp.float32)
+        partial_value.astype(jnp.bfloat16), "dp", scatter_dimension=0, tiled=True
+    )
     output_weight_gradient = lax.psum_scatter(
-        columns.astype(jnp.bfloat16), "seq", scatter_dimension=0, tiled=True
+        columns.T, "seq", scatter_dimension=0, tiled=True
     ).astype(jnp.float32)
     return (latent_block_output, output_weight_gradient)
 

time: 670 us -> 501 us (0.75)
  waiting for transfers between devices: 488 us -> 330 us
  local copies, waits for them, and re-layouts: 63.3 us -> 53.3 us
    all_gather x1, waiting for transfers between devices: 217 us -> 0.02 us  [shards(): weight = lax.all_gather(rows, ('seq', 'dp'), axis=0, tiled=True)]
    all_to_all x1, waiting for transfers between devices: 0.01 us -> 124 us  [shards(): lax.all_to_all(lat_qkv, 'seq', split_axis=3, concat_axis=1, tiled=True)]
    psum x1, waiting for transfers between devices: 153 us -> 88.5 us  [encoder_text(): summed = lax.psum(partial_value, 'seq').astype(jnp.float32)]
    unnamed x13 -> x21, local copies, waits for them, and re-layouts: 33.3 us -> 28.1 us
  transfers between devices with their start and end apart: 5 -> 5, of which waited for: 4 -> 4; matrix products, arithmetic and copies ran while one was open for 4% -> 15% of each run, Pallas kernels for 0% -> 0%
where the time goes in v1:
time: 501 us; the launch traced here: 500 us
  waiting for transfers between devices  330 us (66%)
  matrix products  53.7 us (11%)
  local copies, waits for them, and re-layouts  53.3 us (11%)
  blocking collectives  28.2 us (6%)
  other arithmetic  14.6 us (3%)
  between operations  14.6 us (3%)
  starting transfers between devices  5.21 us (1%)
    all_to_all x1, waiting for transfers between devices, shards(): lax.all_to_all(lat_qkv, 'seq', split_axis=3, concat_axis=1, tiled=True)  124 us
    unnamed x5, waiting for transfers between devices  91.4 us
    psum x1, waiting for transfers between devices, encoder_text(): summed = lax.psum(partial_value, 'seq').astype(jnp.float32)  88.5 us
    all_to_all x1, blocking collectives, shards(): lax.all_to_all(attn_heads, 'seq', split_axis=1, concat_axis=2, tiled=True)  28.2 us
    unnamed x21, local copies, waits for them, and re-layouts  28.1 us
    reduce_scatter x1, waiting for transfers between devices, shards(): lax.psum_scatter(columns.T, 'seq', scatter_dimension=0, tiled=True)  25.8 us
    dot_general x2, matrix products, one_block(): jnp.einsum('shqk,skhd->sqhd', probs, values, preferred_element_type=jnp.f...  12.1 us
  transfers between devices with their start and end apart: 5, of which 4 were waited for; matrix products, arithmetic and copies ran while one was open for 15% of the time, Pallas kernels for 0%

profile of v1, /device:TPU:0, one launch (start us, length us, event | category | flops | bytes accessed | tf_op | source)
XLA Modules:
  0.0 499.8 jit_solution(3858505422608655442)
XLA Ops:
  7.2 8.5 %fusion.47 = bf16[1,256,4096]{2,1,0:T(8,128)(2,1)} fusion(bf16[1280,4096]{1,0:T(8,128)(2,1)} %param.11, bf16[1,256,1280]{2,1,0:T(8,128)(2,1)} %param.10), kind=kOutput, calls=%fused_computation.34 | convolution fusion | flops 2685403136 | bytes 13238272 | tf_op jit(solution)/shard_map/ste,ed->std/dot_general | solution.py:10
  16.6 88.5 %all-reduce.3.cloned.1.call-done = bf16[1,256,4096]{2,1,0:T(8,128)(2,1)} async-done(((bf16[1,256,4096]{2,1,0:T(8,128)(2,1)}), bf16[1,256,4096]{2,1,0:T(8,128)(2,1)}) %all-reduce.3.cloned.1.call-update) | async-done | bytes 2097168 | tf_op jit(solution)/shard_map/psum | solution.py:13
  105.1 2.2 fusion.48
  109.4 7.2 %copy.33 = bf16[1,256,3,2048]{1,2,0,3:T(4,128)(2,1)} copy(bf16[1,256,3,2048]{3,1,2,0:T(8,128)(2,1)} %param.15) | data formatting | bytes 6291456 | tf_op args[5]
  116.5 5.1 %all-to-all-start = ((bf16[1,256,3,2048]{1,2,0,3:T(4,128)(2,1)}), bf16[1,256,3,2048]{1,2,0,3:T(4,128)(2,1)}, u32[]{:S(2)}, u32[]{:S(2)}) async-start(bf16[1,256,3,2048]{1,2,0,3:T(4,128)(2,1)} %copy.33), calls=%async_computation | async-start | bytes 8388608 | tf_op jit(solution)/shard_map/all_to_all | solution.py:59
  122.4 5.7 %fusion.59 = bf16[1,256,2,512]{3,1,2,0:T(8,128)(2,1)S(1)} fusion(bf16[4096,2,512]{2,1,0:T(2,128)(2,1)} %param.14, bf16[1,256,4096]{2,1,0:T(8,128)(2,1)S(1)} %copy-done.4), kind=kOutput, calls=%fused_computation.46 | convolution fusion | flops 2147745792 | bytes 11010048 | tf_op jit(solution)/shard_map/std,dkh->stkh/dot_general | solution.py:56
  129.1 124.3 %all-to-all-done = bf16[1,256,3,2048]{1,2,0,3:T(4,128)(2,1)} async-done(((bf16[1,256,3,2048]{1,2,0,3:T(4,128)(2,1)}), bf16[1,256,3,2048]{1,2,0,3:T(4,128)(2,1)}, u32[]{:S(2)}, u32[]{:S(2)}) %all-to-all-start) | async-done | bytes 3145760 | tf_op jit(solution)/shard_map/all_to_all | solution.py:59
  253.4 5.2 %copy.61 = bf16[1,256,3,4,512]{1,3,4,2,0:T(4,128)(2,1)S(1)} copy(bf16[1,256,3,4,512]{1,2,4,3,0:T(4,128)(2,1)} %bitcast.8) | data formatting | bytes 6291456 | tf_op jit(solution)/shard_map/all_to_all | solution.py:59
  258.6 4.1 all_to_all.29
  262.7 3.3 fusion.72
  272.7 24.0 %while.10 = (s32[]{:T(128)}, bf16[2,1,512,512]{3,2,0,1:T(8,128)(2,1)}, pred[1,1280]{1,0:T(4,128)(4,1)S(1)}, bf16[2,1,512,4,128]{4,2,3,1,0:T(8,128)(2,1)}, bf16[1...) while((s32[]{:T(128)}, bf16[2,1,512,512]{3,2,0,1:T(8,128)(2,1)}, ...), condition=%wide.region_5.6_spmd, body=%wide.region_2.5_spmd.sunk | while | flops 2037125632 | bytes 12866694 | solution.py:44
  272.7 4.8 fusion.88
  277.5 6.1 %fusion.89 = bf16[4,512,128]{1,2,0:T(8,128)(2,1)S(1)} fusion(bf16[1,1280,4,128]{1,3,2,0:T(8,128)(2,1)} %get-tuple-element.136, f32[4,512]{1,0:T(4,128)S(1)} %fusion.88, pred[1280]{0:T(1024)(128)(4,1)S(1)} %reduce.8, bf16[1,1280,4,128]{3,1,2,0:T(8,128)(2,1)S(1)} %copy-done.5, bf16[2,1,512,4,128]{4,2,3,1,0:T(8,128)(2,1)} %get-tuple-element.134, ...), kind=kOutput, calls=%fused_computation.14.clone.1 | convolution fusion | flops 1355549952 | bytes 3679492 | tf_op jit(solution)/shard_map/while/body/eval_jaxpr/shqk,skhd->sqhd/dot_general | solution.py:41
  284.7 4.8 fusion.88
  289.5 6.1 %fusion.89 = bf16[4,512,128]{1,2,0:T(8,128)(2,1)S(1)} fusion(bf16[1,1280,4,128]{1,3,2,0:T(8,128)(2,1)} %get-tuple-element.136, f32[4,512]{1,0:T(4,128)S(1)} %fusion.88, pred[1280]{0:T(1024)(128)(4,1)S(1)} %reduce.8, bf16[1,1280,4,128]{3,1,2,0:T(8,128)(2,1)S(1)} %copy-done.5, bf16[2,1,512,4,128]{4,2,3,1,0:T(8,128)(2,1)} %get-tuple-element.134, ...), kind=kOutput, calls=%fused_computation.14.clone.1 | convolution fusion | flops 1355549952 | bytes 3679492 | tf_op jit(solution)/shard_map/while/body/eval_jaxpr/shqk,skhd->sqhd/dot_general | solution.py:41
  296.6 2.8 copy.62
  300.0 7.0 %reduce.6 = bf16[1024,512]{1,0:T(8,128)(2,1)S(1)} reduce(bf16[1024,1,512]{2,1,0:T(2,128)(2,1)S(1)} %bitcast.111, bf16[]{:T(256)} %broadcast.50), dimensions={1}, to_apply=%bitcast.92.reduce_sub_computation | reduce | bytes 2097154
  307.9 28.2 %all_to_all.36 = bf16[4,2,65536]{2,1,0:T(2,128)(2,1)S(1)} all-to-all(bf16[4,2,65536]{2,1,0:T(2,128)(2,1)S(1)} %reshape.118), channel_id=1, replica_groups=mesh['dp'=8,'seq'=4] {'seq'}, dimensions={0} | all-to-all | bytes 2097152 | tf_op jit(solution)/shard_map/all_to_all | solution.py:61
  337.9 8.2 %convert_bitcast_fusion = bf16[3072,2048]{0,1:T(8,128)(2,1)} fusion(bf16[1,256,3072]{2,1,0:T(8,128)(2,1)} %param.17, bf16[1,256,2048]{1,2,0:T(8,128)(2,1)S(1)} %bitcast.107), kind=kOutput, calls=%fused_computation.28 | convolution fusion | flops 3227516928 | bytes 15204352 | tf_op jit(solution)/shard_map/vwk,vwy->yk/dot_general | solution.py:73
  346.1 15.7 %copy.48 = bf16[3072,2048]{1,0:T(8,128)(2,1)} copy(bf16[3072,2048]{0,1:T(8,128)(2,1)} %convert_bitcast_fusion) | data formatting | bytes 25165824
  361.9 91.4 %reduce-scatter.7.cloned.1.call-done = bf16[384,2048]{1,0:T(8,128)(2,1)} async-done(((bf16[3072,2048]{1,0:T(8,128)(2,1)}), bf16[384,2048]{1,0:T(8,128)(2,1)}) %reduce-scatter.7.cloned.1.call-update) | async-done | bytes 1572880
  453.3 2.6 copy.49
  455.9 9.7 %fusion.51 = bf16[1,256,3072]{2,1,0:T(8,128)(2,1)} fusion(bf16[2048,3072]{1,0:T(8,128)(2,1)} %all-gather.2.cloned.1.call-done, bf16[1,256,2048]{1,2,0:T(8,128)(2,1)} %bitcast.108), kind=kOutput, calls=%fused_computation.39 | convolution fusion | flops 3222011904 | bytes 15204352 | tf_op jit(solution)/shard_map/ugj,jn->ugn/dot_general | solution.py:66
  465.6 25.8 %reduce-scatter.5.cloned.1.call-done = bf16[512,384]{1,0:T(8,128)(2,1)} async-done(((bf16[2048,384]{1,0:T(8,128)(2,1)}), bf16[512,384]{1,0:T(8,128)(2,1)}) %reduce-scatter.5.cloned.1.call-update) | async-done | bytes 393232 | tf_op jit(solution)/shard_map/reduce_scatter | solution.py:79
  (53 shorter events, 17.9 us)
Async XLA Ops:
  7.2 8.6 %copy-start = (bf16[512,3072]{1,0:T(8,128)(2,1)S(1)}, bf16[512,3072]{1,0:T(8,128)(2,1)}, u32[]{:S(2)}) copy-start(bf16[512,3072]{1,0:T(8,128)(2,1)} %param.16) | copy-start | bytes 9437188
  7.2 97.9 %all-reduce.3.cloned.1.call-start = ((), (), s32[]{:S(2)}) async-start(), calls=%async_computation.4 | async-start | bytes 4194304 | tf_op jit(solution)/shard_map/psum | solution.py:13
  15.7 91.6 %copy-start.7 = (f32[4096]{0:T(1024)S(1)}, f32[4096]{0:T(1024)}, u32[]{:S(2)}) copy-start(f32[4096]{0:T(1024)} %param.12) | copy-start | bytes 49156
  15.8 322.2 %all-gather.2.cloned.1.call-start = ((), (), s32[]{:S(2)}) async-start(), calls=%async_computation.5 | async-start | bytes 12976128 | tf_op jit(solution)/shard_map/all_gather | solution.py:55
  105.1 2.3 copy-start.3
  116.5 5.8 %copy-start.4 = (bf16[1,256,4096]{2,1,0:T(8,128)(2,1)S(1)}, bf16[1,256,4096]{2,1,0:T(8,128)(2,1)}, u32[]{:S(2)}) copy-start(bf16[1,256,4096]{2,1,0:T(8,128)(2,1)} %fusion.50) | copy-start | bytes 6291460
  116.5 136.9 %all-to-all-start = ((bf16[1,256,3,2048]{1,2,0,3:T(4,128)(2,1)}), bf16[1,256,3,2048]{1,2,0,3:T(4,128)(2,1)}, u32[]{:S(2)}, u32[]{:S(2)}) async-start(bf16[1,256,3,2048]{1,2,0,3:T(4,128)(2,1)} %copy.33), calls=%async_computation | async-start | bytes 8388608 | tf_op jit(solution)/shard_map/all_to_all | solution.py:59
  121.6 331.7 %reduce-scatter.7.cloned.1.call-start = ((), (), s32[]{:S(2)}) async-start(), calls=%async_computation.7 | async-start | bytes 14155776
  262.7 3.3 copy-start.6
  272.7 4.8 copy-start.5
  284.7 4.8 copy-start.5
  337.9 8.2 %copy-start.2 = (bf16[1,256,4,512]{1,3,2,0:T(8,128)(2,1)}, bf16[1,256,4,512]{1,3,2,0:T(8,128)(2,1)S(1)}, u32[]{:S(2)}) copy-start(bf16[1,256,4,512]{1,3,2,0:T(8,128)(2,1)S(1)} %copy.43) | copy-start | bytes 3145732
  361.8 129.5 %reduce-scatter.5.cloned.1.call-start = ((), (), s32[]{:S(2)}) async-start(), calls=%async_computation.6 | async-start | bytes 1966080 | tf_op jit(solution)/shard_map/reduce_scatter | solution.py:79
  455.9 37.4 %copy-start.1 = (bf16[512,3072]{1,0:T(8,128)(2,1)S(1)}, bf16[512,3072]{1,0:T(8,128)(2,1)}, u32[]{:S(2)}) copy-start(bf16[512,3072]{1,0:T(8,128)(2,1)} %param.16) | copy-start | bytes 9437188
Sparse Core Ops, SparseCore 0:
  15.9 89.2 all-reduce.2
  109.5 163.9 all-gather.1
  362.0 91.2 reduce-scatter.6
  456.0 35.2 reduce-scatter.4

commit v2 on v0

v2 whole, which is shorter than its diff:
```python
import functools
import math

import jax
import jax.numpy as jnp
from jax import lax
from jax.experimental import pallas as pl
from jax.experimental.pallas import tpu as pltpu
from jax.sharding import PartitionSpec as P

HD = 128
MESH = pl.DeviceIdType.MESH
ANY = pl.BlockSpec(memory_space=pl.ANY)


def collect_kernel(n, chips, qkv, rows, heads, weight, z_s, z_r, q_s, q_r, p_s, p_r, c_s, c_r, own):
    me, dp = lax.axis_index("seq"), lax.axis_index("dp")
    chip, core = dp // 2, dp % 2
    other = 2 * chip + 1 - core
    tokens = qkv.shape[1]
    width = heads.shape[2]
    block = rows.shape[0]
    share = block // (2 * chips)

    barrier = pltpu.get_barrier_semaphore()
    for k in range(1, n):
        to = lax.rem(me + k, n)
        pl.semaphore_signal(barrier, inc=1, device_id=(dp, to), device_id_type=MESH)
    for k in range(1, chips):
        to = 2 * lax.rem(chip + k, chips) + core
        pl.semaphore_signal(barrier, inc=1, device_id=(to, me), device_id_type=MESH)
    pl.semaphore_signal(barrier, inc=1, device_id=(other, me), device_id_type=MESH)
    pl.semaphore_wait(barrier, n - 1 + chips - 1 + 1)

    def remote(src, dst, send, recv, to):
        return pltpu.make_async_remote_copy(
            src_ref=src, dst_ref=dst, send_sem=send, recv_sem=recv, device_id=to, device_id_type=MESH
        )

    def piece(s, d):
        start = pl.multiple_of(s * block + d * share, share)
        return weight.at[pl.ds(start, share)]

    def columns(s):
        return pl.ds(pl.multiple_of(s * width, width), width)

    mine = pl.ds(pl.multiple_of(me * tokens, tokens), tokens)
    fetch, tokens_out = [], []
    for k in range(1, n):
        to = lax.rem(me + k, n)
        fetch.append(
            remote(
                rows.at[pl.ds(pl.multiple_of(dp * share, share), share)],
                piece(me, dp), z_s.at[k - 1], z_r.at[k - 1], (dp, to),
            )
        )
        fetch[-1].start()
    for k in range(1, n):
        to = lax.rem(me + k, n)
        tokens_out.append(
            remote(
                qkv.at[:, :, columns(to)], heads.at[:, mine], q_s.at[k - 1], q_r.at[k - 1], (dp, to)
            )
        )
        tokens_out[-1].start()
    stay = [
        pltpu.make_async_copy(qkv.at[:, :, columns(me)], heads.at[:, mine], own.at[0]),
        pltpu.make_async_copy(
            rows, weight.at[pl.ds(pl.multiple_of(me * block, block), block)], own.at[1]
        ),
    ]
    for copy in stay:
        copy.start()

    plane, cores = [], []
    for k in range(1, n):
        fetch[k - 1].wait_recv()
        source = lax.rem(me - k + n, n)
        held = piece(source, dp)
        for c in range(1, chips):
            to = 2 * lax.rem(chip + c, chips) + core
            plane.append(remote(held, held, p_s.at[k - 1, c - 1], p_r.at[k - 1, c - 1], (to, me)))
            plane[-1].start()
        cores.append(remote(held, held, c_s.at[k - 1, 0], c_r.at[k - 1, 0], (other, me)))
        cores[-1].start()
    for k in range(1, n):
        source = lax.rem(me - k + n, n)
        for c in range(1, chips):
            plane[(k - 1) * (chips - 1) + c - 1].wait_recv()
            held = piece(source, 2 * lax.rem(chip - c + chips, chips) + core)
            cores.append(remote(held, held, c_s.at[k - 1, c], c_r.at[k - 1, c], (other, me)))
            cores[-1].start()
    for copy in fetch + plane:
        copy.wait_send()
    for copy in cores + tokens_out + stay:
        copy.wait()


def collect(lat_qkv, output_weight):
    n, chips = lax.axis_size("seq"), lax.axis_size("dp") // 2
    _, tokens, _, wide = lat_qkv.shape
    block, features = output_weight.shape
    dma = pltpu.SemaphoreType.DMA
    return pl.pallas_call(
        functools.partial(collect_kernel, n, chips),
        out_shape=(
            jax.ShapeDtypeStruct((3, n * tokens, wide // n), lat_qkv.dtype),
            jax.ShapeDtypeStruct((n * block, features), output_weight.dtype),
        ),
        in_specs=[ANY, ANY],
        out_specs=(ANY, ANY),
        scratch_shapes=[
            dma((n - 1,)), dma((n - 1,)), dma((n - 1,)), dma((n - 1,)),
            dma((n - 1, chips - 1)), dma((n - 1, chips - 1)),
            dma((n - 1, chips)), dma((n - 1, chips)), dma((2,)),
        ],
        compiler_params=pltpu.CompilerParams(collective_id=0, has_side_effects=True),
        cost_estimate=pl.CostEstimate(flops=0, bytes_accessed=300_000_000, transcendentals=0),
    )(jnp.transpose(lat_qkv[0], (1, 0, 2)), output_weight)


def return_kernel(n, attn, rows, send, recv, own):
    me, dp = lax.axis_index("seq"), lax.axis_index("dp")
    tokens, width = rows.shape[0], attn.shape[1]
    barrier = pltpu.get_barrier_semaphore()
    for k in range(1, n):
        to = lax.rem(me + k, n)
        pl.semaphore_signal(barrier, inc=1, device_id=(dp, to), device_id_type=MESH)
    pl.semaphore_wait(barrier, n - 1)
    mine = rows.at[:, pl.ds(pl.multiple_of(me * width, width), width)]

    def part(s):
        return attn.at[pl.ds(pl.multiple_of(s * tokens, tokens), tokens)]

    copies = []
    for k in range(1, n):
        to = lax.rem(me + k, n)
        copies.append(
            pltpu.make_async_remote_copy(
                src_ref=part(to), dst_ref=mine, send_sem=send.at[k - 1], recv_sem=recv.at[k - 1],
                device_id=(dp, to), device_id_type=MESH,
            )
        )
    copies.append(pltpu.make_async_copy(part(me), mine, own))
    for copy in copies:
        copy.start()
    for copy in copies:
        copy.wait()


def give_back(attn):
    n = lax.axis_size("seq")
    latent, width = attn.shape
    dma = pltpu.SemaphoreType.DMA
    return pl.pallas_call(
        functools.partial(return_kernel, n),
        out_shape=jax.ShapeDtypeStruct((latent // n, width * n), attn.dtype),
        in_specs=[ANY],
        out_specs=ANY,
        scratch_shapes=[dma((n - 1,)), dma((n - 1,)), dma],
        compiler_params=pltpu.CompilerParams(collective_id=1, has_side_effects=True),
        cost_estimate=pl.CostEstimate(flops=0, bytes_accessed=60_000_000, transcendentals=0),
    )(attn)


def attend_kernel(length, q, k, v, text_k, text_v, out):
    turned = (((1,), (1,)), ((), ()))
    query = q[0]
    latent = lax.dot_general(query, k[0], turned, preferred_element_type=jnp.float32)
    text = lax.dot_general(query, text_k[0], turned, preferred_element_type=jnp.float32)
    place = lax.broadcasted_iota(jnp.int32, text.shape, 1)
    text = jnp.where(place < length[0], text, -1e30)
    top = jnp.maximum(jnp.max(latent, -1, keepdims=True), jnp.max(text, -1, keepdims=True))
    scale = HD ** (-0.5) * math.log2(math.e)
    latent = jnp.exp2((latent - top) * scale)
    text = jnp.exp2((text - top) * scale)
    total = jnp.sum(latent, -1, keepdims=True) + jnp.sum(text, -1, keepdims=True)
    result = jnp.dot(latent.astype(jnp.bfloat16), v[0], preferred_element_type=jnp.float32)
    result += jnp.dot(text.astype(jnp.bfloat16), text_v[0], preferred_element_type=jnp.float32)
    out[...] = (result / total).astype(out.dtype)


def attend(heads, text, text_len):
    _, latent, width = heads.shape
    count = text.shape[1]
    rows = min(512, latent)

    def block(index, size):
        return pl.BlockSpec((1, size, HD), lambda h, i: (index, 0, h))

    return pl.pallas_call(
        attend_kernel,
        grid=(width // HD, latent // rows),
        in_specs=[
            pl.BlockSpec(memory_space=pltpu.SMEM),
            pl.BlockSpec((1, rows, HD), lambda h, i: (0, i, h)),
            block(1, latent), block(2, latent), block(0, count), block(1, count),
        ],
        out_specs=pl.BlockSpec((rows, HD), lambda h, i: (i, h)),
        out_shape=jax.ShapeDtypeStruct((latent, width), jnp.bfloat16),
        compiler_params=pltpu.CompilerParams(vmem_limit_bytes=40 * 2**20),
    )(text_len, heads, heads, heads, text, text)


def gradient_kernel(attn, cotangent, out):
    product = lax.dot_general(
        attn[...], cotangent[...], (((0,), (0,)), ((), ())), preferred_element_type=jnp.float32
    ).astype(out.dtype)
    width = out.shape[2]
    for part in range(out.shape[0]):
        out[part] = product[:, part * width : (part + 1) * width]


def gradient(attn, cotangent, parts):
    tokens, wide = attn.shape
    features = cotangent.shape[1]
    width = features // parts
    rows = min(256, wide)
    return pl.pallas_call(
        gradient_kernel,
        grid=(wide // rows,),
        in_specs=[
            pl.BlockSpec((tokens, rows), lambda r: (0, r)),
            pl.BlockSpec((tokens, features), lambda r: (0, 0)),
        ],
        out_specs=pl.BlockSpec((parts, rows, width), lambda r: (0, r, 0)),
        out_shape=jax.ShapeDtypeStruct((parts, wide, width), jnp.bfloat16),
        compiler_params=pltpu.CompilerParams(vmem_limit_bytes=40 * 2**20),
    )(attn, cotangent)


def shards(
    enc_hidden, enc_wo, enc_gain, text_len, text_kv, lat_qkv, output_weight, output_cotangent
):
    partial_value = jnp.dot(
        enc_hidden[0], enc_wo, preferred_element_type=jnp.float32
    ).astype(jnp.bfloat16)
    partial_value, lat_qkv = lax.optimization_barrier((partial_value, lat_qkv))
    summed = lax.psum(partial_value, "seq")
    heads, weight = collect(lat_qkv, output_weight)
    summed = summed.astype(jnp.float32)
    meansq = jnp.mean(summed * summed, -1, keepdims=True)
    text_emb = (summed * lax.rsqrt(meansq + 1e-06) * enc_gain).astype(jnp.bfloat16)
    text = jnp.einsum(
        "td,dkh->kth", text_emb, text_kv, preferred_element_type=jnp.float32
    ).astype(jnp.bfloat16)
    rows = give_back(attend(heads, text, text_len))
    parts = gradient(rows, output_cotangent[0], lax.axis_size("dp"))
    columns = lax.psum_scatter(parts, "dp", scatter_dimension=0, tiled=False)
    output_weight_gradient = lax.psum_scatter(
        columns, "seq", scatter_dimension=0, tiled=True
    ).astype(jnp.float32)
    projected = jnp.dot(rows, weight, preferred_element_type=jnp.float32)
    return (projected.astype(jnp.bfloat16)[None], output_weight_gradient)


def solution(mesh):
    placed = (
        P("dp", None, "seq"),
        P("seq", None),
        P(),
        P("dp"),
        P(None, None, "seq"),
        P("dp", "seq", None, None),
        P("seq", None),
        P("dp", "seq", None),
    )
    return jax.shard_map(
        shards,
        mesh=mesh,
        in_specs=placed,
        out_specs=(P("dp", "seq", None), P("seq", "dp")),
        check_vma=False,
    )
```

time: 670 us -> 391 us (0.58)
  waiting for transfers between devices: 488 us -> 144 us
  Pallas kernels: 0 us -> 201 us
  local copies, waits for them, and re-layouts: 63.3 us -> 3.24 us
  blocking collectives: 29.7 us -> 0 us
  matrix products: 52.3 us -> 23.7 us
  other arithmetic: 14.6 us -> 4.02 us
    all_gather x1 -> x0, waiting for transfers between devices: 217 us -> none  [shards(): lax.all_gather(output_weight, 'seq', axis=0, tiled=True)]
    pallas_call x0 -> x4, Pallas kernels: none -> 201 us  [the longest x1 150 us: collect(): pl.pallas_call(functools.partial(collect_kernel, n, chips), out_shape=(ja...]
    psum x1, waiting for transfers between devices: 153 us -> 18.2 us  [shards(): summed = lax.psum(partial_value, 'seq')]
    reduce_scatter x1 -> x2, waiting for transfers between devices: 26.6 us -> 125 us  [the longest x1 96.6 us: shards(): columns = lax.psum_scatter(parts, 'dp', scatter_dimension=0, tiled=False)]
    unnamed x5 -> x3, waiting for transfers between devices: 91.6 us -> 0.05 us
    unnamed x13 -> x14, local copies, waits for them, and re-layouts: 33.3 us -> 3.24 us
    all_to_all x1 -> x0, blocking collectives: 29.7 us -> none  [shards(): lax.all_to_all(attn_heads, 'seq', split_axis=1, concat_axis=2, tiled=True)]
    dot_general x6 -> x3, matrix products: 42.9 us -> 23.7 us  [the longest x1 9.09 us: shards(): projected = jnp.dot(rows, weight, preferred_element_type=jnp.float32)]
  transfers between devices with their start and end apart: 5 -> 3, of which waited for: 4 -> 3; matrix products, arithmetic and copies ran while one was open for 4% -> 2% of each run, Pallas kernels for 0% -> 39%
where the time goes in v2:
time: 391 us; the launch traced here: 390 us
  Pallas kernels  201 us (51%)
  waiting for transfers between devices  144 us (37%)
  matrix products  23.7 us (6%)
  between operations  14.5 us (4%)
  other arithmetic  4.02 us (1%)
    pallas_call x1, Pallas kernels, collect(): pl.pallas_call(functools.partial(collect_kernel, n, chips), out_shape=(ja...  150 us
    reduce_scatter x1, waiting for transfers between devices, shards(): columns = lax.psum_scatter(parts, 'dp', scatter_dimension=0, tiled=False)  96.6 us
    reduce_scatter x1, waiting for transfers between devices, shards(): lax.psum_scatter(columns, 'seq', scatter_dimension=0, tiled=True)  28.6 us
    pallas_call x1, Pallas kernels, give_back(): pl.pallas_call(functools.partial(return_kernel, n), out_shape=jax.ShapeDt...  28.2 us
    psum x1, waiting for transfers between devices, shards(): summed = lax.psum(partial_value, 'seq')  18.2 us
    pallas_call x1, Pallas kernels, attend(): pl.pallas_call(attend_kernel, grid=(width // HD, latent // rows), in_spec...  14.8 us
    dot_general x1, matrix products, shards(): projected = jnp.dot(rows, weight, preferred_element_type=jnp.float32)  9.09 us
    dot_general x1, matrix products, shards(): jnp.dot(enc_hidden[0], enc_wo, preferred_element_type=jnp.float32)  8.05 us
  transfers between devices with their start and end apart: 3, of which 3 were waited for; matrix products, arithmetic and copies ran while one was open for 2% of the time, Pallas kernels for 39%

profile of v2, /device:TPU:0, one launch (start us, length us, event | category | flops | bytes accessed | tf_op | source)
XLA Modules:
  0.0 390.1 jit_solution(3804347721619577347)
XLA Ops:
  7.2 0.0 copy-start
  7.2 0.0 all-reduce.2.cloned.1.call-start
  7.2 1.0 copy-done
  8.3 8.1 %convolution_convert_fusion = bf16[256,4096]{1,0:T(8,128)(2,1)} fusion(bf16[1280,4096]{1,0:T(8,128)(2,1)} %param.9, bf16[1,256,1280]{2,1,0:T(8,128)(2,1)S(1)} %copy-done), kind=kOutput, calls=%fused_computation.4 | convolution fusion | flops 2685403136 | bytes 13238272 | tf_op jit(solution)/shard_map/dot_general | solution.py:235
  16.3 0.0 all-reduce.2.cloned.1.call-update
  16.3 0.0 reduce-scatter.3.cloned.1.call-start
  17.0 0.0 copy-start.6
  17.0 150.2 %shard_map.95 = (bf16[3,1024,512]{2,1,0:T(8,128)(2,1)}, bf16[2048,3072]{1,0:T(8,128)(2,1)}) custom-call(bf16[3,256,2048]{2,1,0:T(8,128)(2,1)} %bitcast.23, bf16[512,3072]{1,0:T(8,128)(2,1)} %rows.1), custom_call_target="tpu_custom_call" | custom-call | bytes 300000000 | tf_op jit(solution)/shard_map/pallas_call | solution.py:104
  167.3 18.2 %all-reduce.2.cloned.1.call-done = bf16[256,4096]{1,0:T(8,128)(2,1)} async-done(((bf16[256,4096]{1,0:T(8,128)(2,1)}), bf16[256,4096]{1,0:T(8,128)(2,1)}) %all-reduce.2.cloned.1.call-update) | async-done | bytes 2097168 | tf_op jit(solution)/shard_map/psum | solution.py:239
  185.5 2.1 fusion.2
  187.6 6.5 %fusion.15.text_k.text_v = bf16[2,256,512]{2,1,0:T(8,128)(2,1)S(1)} fusion(bf16[4096,2,512]{2,1,0:T(2,128)(2,1)} %param.12, bf16[256,4096]{1,0:T(8,128)(2,1)} %all-reduce.2.cloned.1.call-done, f32[4096]{0:T(1024)S(1)} %copy-done.6, f32[256]{0:T(256)S(1)} %add_rsqrt_fusion), kind=kOutput, calls=%fused_computation.14 | convolution fusion | flops 2151940096 | bytes 11027456 | tf_op jit(solution)/shard_map/td,dkh->kth/dot_general | solution.py:244
  194.2 0.0 copy-start.5
  194.2 14.8 %shard_map.96.attn = bf16[1024,512]{1,0:T(8,128)(2,1)S(1)} custom-call(s32[1]{0:T(128)S(6)} %copy.18.length, bf16[3,1024,512]{2,1,0:T(8,128)(2,1)S(1)} %copy-done.1, bf16[3,1024,512]{2,1,0:T(8,128)(2,1)S(1)} %copy-done.1, bf16[3,1024,512]{2,1,0:T(8,128)(2,1)S(1)} %copy-done.1, bf16[2,256,512]{2,1,0:T(8,128)(2,1)S(1)} %fusion.15.text_k.text_v, ...), custom_call_target="tpu_custom_call" | custom-call | tf_op jit(solution)/shard_map/pallas_call | solution.py:191
  209.0 1.0 copy-done.2
  210.0 28.2 %shard_map.97.attn = bf16[256,2048]{1,0:T(8,128)(2,1)} custom-call(bf16[1024,512]{1,0:T(8,128)(2,1)} %copy-done.2), custom_call_target="tpu_custom_call" | custom-call | bytes 60000000 | tf_op jit(solution)/shard_map/pallas_call | solution.py:155
  238.2 1.2 copy-done.3
  239.4 7.8 %shard_map.98 = bf16[8,2048,384]{2,1,0:T(8,128)(2,1)} custom-call(bf16[256,2048]{1,0:T(8,128)(2,1)S(1)} %copy-done.3, bf16[256,3072]{1,0:T(8,128)(2,1)S(1)} %bitcast.22), custom_call_target="tpu_custom_call" | custom-call | tf_op jit(solution)/shard_map/pallas_call | solution.py:219
  247.3 0.0 reduce-scatter.3.cloned.1.call-update
  247.3 0.0 reduce-scatter.5.cloned.1.call-start
  247.3 96.6 %reduce-scatter.3.cloned.1.call-done = bf16[1,2048,384]{2,1,0:T(8,128)(2,1)} async-done(((bf16[8,2048,384]{2,1,0:T(8,128)(2,1)}), bf16[1,2048,384]{2,1,0:T(8,128)(2,1)}) %reduce-scatter.3.cloned.1.call-update) | async-done | bytes 1572880 | tf_op jit(solution)/shard_map/reduce_scatter | solution.py:249
  344.0 0.0 reduce-scatter.5.cloned.1.call-update
  344.0 9.1 %fusion.5 = bf16[1,256,3072]{2,1,0:T(8,128)(2,1)} fusion(bf16[256,2048]{1,0:T(8,128)(2,1)S(1)} %copy-done.4, bf16[2048,3072]{1,0:T(8,128)(2,1)} %get-tuple-element.9), kind=kOutput, calls=%fused_computation.9 | convolution fusion | flops 3222011904 | bytes 15204352 | tf_op jit(solution)/shard_map/dot_general | solution.py:253
  353.1 28.6 %reduce-scatter.5.cloned.1.call-done = bf16[512,384]{1,0:T(8,128)(2,1)} async-done(((bf16[2048,384]{1,0:T(8,128)(2,1)}), bf16[512,384]{1,0:T(8,128)(2,1)}) %reduce-scatter.5.cloned.1.call-update) | async-done | bytes 393232 | tf_op jit(solution)/shard_map/reduce_scatter | solution.py:250
  381.7 1.9 convert_element_type.26
  (9 shorter events, 0.0 us)
Async XLA Ops:
  7.2 1.1 copy-start
  7.2 178.3 %all-reduce.2.cloned.1.call-start = ((), (), s32[]{:S(2)}) async-start(), calls=%async_computation.2 | async-start | bytes 4194304 | tf_op jit(solution)/shard_map/psum | solution.py:239
  16.3 327.6 %reduce-scatter.3.cloned.1.call-start = ((), (), s32[]{:S(2)}) async-start(), calls=%async_computation.3 | async-start | bytes 14155776 | tf_op jit(solution)/shard_map/reduce_scatter | solution.py:249
  17.0 170.6 %copy-start.6 = (f32[4096]{0:T(1024)S(1)}, f32[4096]{0:T(1024)}, u32[]{:S(2)}) copy-start(f32[4096]{0:T(1024)} %param.10) | copy-start | bytes 49156
  187.6 6.6 %copy-start.1 = (bf16[3,1024,512]{2,1,0:T(8,128)(2,1)S(1)}, bf16[3,1024,512]{2,1,0:T(8,128)(2,1)}, u32[]{:S(2)}) copy-start(bf16[3,1024,512]{2,1,0:T(8,128)(2,1)} %get-tuple-element.7.q.k.v) | copy-start | bytes 9437188
  194.2 44.0 %copy-start.5 = (bf16[1,256,3072]{2,1,0:T(8,128)(2,1)S(1)}, bf16[1,256,3072]{2,1,0:T(8,128)(2,1)}, u32[]{:S(2)}) copy-start(bf16[1,256,3072]{2,1,0:T(8,128)(2,1)} %param.15) | copy-start | bytes 4718596
  209.0 1.0 copy-start.2
  238.2 1.2 copy-start.3
  247.2 96.7 %copy-start.4 = (bf16[256,2048]{1,0:T(8,128)(2,1)S(1)}, bf16[256,2048]{1,0:T(8,128)(2,1)}, u32[]{:S(2)}) copy-start(bf16[256,2048]{1,0:T(8,128)(2,1)} %shard_map.97.attn) | copy-start | bytes 3145732
  247.3 134.4 %reduce-scatter.5.cloned.1.call-start = ((), (), s32[]{:S(2)}) async-start(), calls=%async_computation.4 | async-start | bytes 1966080 | tf_op jit(solution)/shard_map/reduce_scatter | solution.py:250
Sparse Core Ops, SparseCore 0:
  16.5 169.0 all-reduce.1
  247.4 96.5 reduce-scatter.2
  346.4 35.2 reduce-scatter.4

commit v3 on v2

--- a/solution.py
+++ b/solution.py
@@ -202,30 +202,100 @@
     )(text_len, heads, heads, heads, text, text)
 
 
-def gradient_kernel(attn, cotangent, out):
-    product = lax.dot_general(
-        attn[...], cotangent[...], (((0,), (0,)), ((), ())), preferred_element_type=jnp.float32
-    ).astype(out.dtype)
-    width = out.shape[2]
-    for part in range(out.shape[0]):
-        out[part] = product[:, part * width : (part + 1) * width]
-
-
-def gradient(attn, cotangent, parts):
+def gradient_kernel(
+    chips, attn, cotangent, out, turned, give, got, keep, land, g_s, g_r, k_s, k_r
+):
+    me, dp = lax.axis_index("seq"), lax.axis_index("dp")
+    chip, core = dp // 2, dp % 2
+    other = 2 * chip + 1 - core
+    wide = out.shape[0]
+    tile = math.gcd(wide, 512)
+
+    barrier = pltpu.get_barrier_semaphore()
+    for k in range(1, chips):
+        to = 2 * lax.rem(chip + k, chips) + core
+        pl.semaphore_signal(barrier, inc=1, device_id=(to, me), device_id_type=MESH)
+    pl.semaphore_signal(barrier, inc=1, device_id=(other, me), device_id_type=MESH)
+    turned[...] = attn[...].T
+    pl.semaphore_wait(barrier, chips)
+
+    def remote(src, dst, send, recv, to):
+        return pltpu.make_async_remote_copy(
+            src_ref=src, dst_ref=dst, send_sem=send, recv_sem=recv, device_id=to, device_id_type=MESH
+        )
+
+    def tiles(body):
+        def step(t, carry):
+            body(pl.ds(pl.multiple_of(t * tile, tile), tile))
+            return carry
+
+        lax.fori_loop(0, wide // tile, step, 0)
+
+    def term(rows, index):
+        return jnp.dot(turned[rows, :], cotangent[index], preferred_element_type=jnp.float32)
+
+    order = list(range(1, chips)) + [0]
+    gives, keeps = {}, []
+    for k in order:
+        index = 2 * lax.rem(chip + k, chips) + 1 - core
+
+        def fill(rows):
+            give[k, rows, :] = term(rows, index).astype(give.dtype)
+
+        tiles(fill)
+        gives[k] = remote(give.at[k], got.at[k], g_s.at[k], g_r.at[k], (other, me))
+        gives[k].start()
+    for k in range(1, chips):
+        index = 2 * lax.rem(chip + k, chips) + core
+        gives[k].wait_recv()
+
+        def add(rows):
+            both = term(rows, index) + got[k, rows, :].astype(jnp.float32)
+            keep[k - 1, rows, :] = both.astype(keep.dtype)
+
+        tiles(add)
+        keeps.append(remote(keep.at[k - 1], land.at[k - 1], k_s.at[k - 1], k_r.at[k - 1], (index, me)))
+        keeps[-1].start()
+    gives[0].wait_recv()
+    for copy in keeps:
+        copy.wait_recv()
+
+    def finish(rows):
+        total = term(rows, dp) + got[0, rows, :].astype(jnp.float32)
+        for k in range(1, chips):
+            total += land[k - 1, rows, :].astype(jnp.float32)
+        out[rows, :] = total.astype(out.dtype)
+
+    tiles(finish)
+    for copy in list(gives.values()) + keeps:
+        copy.wait_send()
+
+
+def gradient(attn, cotangent):
+    parts = lax.axis_size("dp")
+    chips = parts // 2
     tokens, wide = attn.shape
-    features = cotangent.shape[1]
-    width = features // parts
-    rows = min(256, wide)
+    width = cotangent.shape[1] // parts
+    cotangent = jnp.transpose(cotangent.reshape(tokens, parts, width), (1, 0, 2))
+    vmem = pl.BlockSpec(memory_space=pltpu.VMEM)
+    dma = pltpu.SemaphoreType.DMA
     return pl.pallas_call(
-        gradient_kernel,
-        grid=(wide // rows,),
-        in_specs=[
-            pl.BlockSpec((tokens, rows), lambda r: (0, r)),
-            pl.BlockSpec((tokens, features), lambda r: (0, 0)),
+        functools.partial(gradient_kernel, chips),
+        in_specs=[vmem, vmem],
+        out_specs=vmem,
+        out_shape=jax.ShapeDtypeStruct((wide, width), jnp.bfloat16),
+        scratch_shapes=[
+            pltpu.VMEM((wide, tokens), jnp.bfloat16),
+            pltpu.VMEM((chips, wide, width), jnp.bfloat16),
+            pltpu.VMEM((chips, wide, width), jnp.bfloat16),
+            pltpu.VMEM((chips - 1, wide, width), jnp.bfloat16),
+            pltpu.VMEM((chips - 1, wide, width), jnp.bfloat16),
+            dma((chips,)), dma((chips,)), dma((chips - 1,)), dma((chips - 1,)),
         ],
-        out_specs=pl.BlockSpec((parts, rows, width), lambda r: (0, r, 0)),
-        out_shape=jax.ShapeDtypeStruct((parts, wide, width), jnp.bfloat16),
-        compiler_params=pltpu.CompilerParams(vmem_limit_bytes=40 * 2**20),
+        compiler_params=pltpu.CompilerParams(
+            collective_id=2, has_side_effects=True, vmem_limit_bytes=52 * 2**20
+        ),
+        cost_estimate=pl.CostEstimate(flops=0, bytes_accessed=200_000_000, transcendentals=0),
     )(attn, cotangent)
 
 
@@ -238,6 +308,7 @@
     partial_value, lat_qkv = lax.optimization_barrier((partial_value, lat_qkv))
     summed = lax.psum(partial_value, "seq")
     heads, weight = collect(lat_qkv, output_weight)
+    heads, output_cotangent = lax.optimization_barrier((heads, output_cotangent))
     summed = summed.astype(jnp.float32)
     meansq = jnp.mean(summed * summed, -1, keepdims=True)
     text_emb = (summed * lax.rsqrt(meansq + 1e-06) * enc_gain).astype(jnp.bfloat16)
@@ -245,8 +316,7 @@
         "td,dkh->kth", text_emb, text_kv, preferred_element_type=jnp.float32
     ).astype(jnp.bfloat16)
     rows = give_back(attend(heads, text, text_len))
-    parts = gradient(rows, output_cotangent[0], lax.axis_size("dp"))
-    columns = lax.psum_scatter(parts, "dp", scatter_dimension=0, tiled=False)
+    columns = gradient(rows, output_cotangent[0])
     output_weight_gradient = lax.psum_scatter(
         columns, "seq", scatter_dimension=0, tiled=True
     ).astype(jnp.float32)

time: 391 us -> 374 us (0.957)
  waiting for transfers between devices: 144 us -> 46.4 us
  Pallas kernels: 201 us -> 278 us
    reduce_scatter x1 -> x0, waiting for transfers between devices: 96.6 us -> none  [shards(): columns = lax.psum_scatter(parts, 'dp', scatter_dimension=0, tiled=False)]
    pallas_call x1, Pallas kernels: 7.82 us -> 81.3 us  [gradient(): pl.pallas_call(functools.partial(gradient_kernel, chips), in_specs=[vmem,...]
  transfers between devices with their start and end apart: 3 -> 2, of which waited for: 3 -> 2; matrix products, arithmetic and copies ran while one was open for 2% -> 3% of each run, Pallas kernels for 39% -> 40%
where the time goes in v3:
time: 374 us; the launch traced here: 373 us
  Pallas kernels  278 us (74%)
  waiting for transfers between devices  46.4 us (12%)
  matrix products  23.7 us (6%)
  between operations  14.8 us (4%)
  local copies, waits for them, and re-layouts  6.57 us (2%)
  other arithmetic  4.02 us (1%)
    pallas_call x1, Pallas kernels, collect(): pl.pallas_call(functools.partial(collect_kernel, n, chips), out_shape=(ja...  150 us
    pallas_call x1, Pallas kernels, gradient(): pl.pallas_call(functools.partial(gradient_kernel, chips), in_specs=[vmem,...  81.3 us
    pallas_call x1, Pallas kernels, give_back(): pl.pallas_call(functools.partial(return_kernel, n), out_shape=jax.ShapeDt...  31.4 us
    reduce_scatter x1, waiting for transfers between devices, shards(): lax.psum_scatter(columns, 'seq', scatter_dimension=0, tiled=True)  31.4 us
    psum x1, waiting for transfers between devices, shards(): summed = lax.psum(partial_value, 'seq')  14.9 us
    pallas_call x1, Pallas kernels, attend(): pl.pallas_call(attend_kernel, grid=(width // HD, latent // rows), in_spec...  14.8 us
    dot_general x1, matrix products, shards(): projected = jnp.dot(rows, weight, preferred_element_type=jnp.float32)  9.09 us
    dot_general x1, matrix products, shards(): jnp.dot(enc_hidden[0], enc_wo, preferred_element_type=jnp.float32)  8.06 us
  transfers between devices with their start and end apart: 2, of which 2 were waited for; matrix products, arithmetic and copies ran while one was open for 3% of the time, Pallas kernels for 40%

profile of v3, /device:TPU:0, one launch (start us, length us, event | category | flops | bytes accessed | tf_op | source)
XLA Modules:
  0.0 373.3 jit_solution(6368953907956453859)
XLA Ops:
  7.2 0.0 copy-start
  7.2 0.0 all-reduce.2.cloned.1.call-start
  7.2 1.0 copy-done
  8.3 8.1 %convolution_convert_fusion = bf16[256,4096]{1,0:T(8,128)(2,1)} fusion(bf16[1280,4096]{1,0:T(8,128)(2,1)} %param.9, bf16[1,256,1280]{2,1,0:T(8,128)(2,1)S(1)} %copy-done), kind=kOutput, calls=%fused_computation.4 | convolution fusion | flops 2685403136 | bytes 13238272 | tf_op jit(solution)/shard_map/dot_general | solution.py:305
  16.3 0.0 all-reduce.2.cloned.1.call-update
  16.3 0.0 reduce-scatter.2.cloned.1.call-start
  17.0 150.2 %shard_map.95 = (bf16[3,1024,512]{2,1,0:T(8,128)(2,1)}, bf16[2048,3072]{1,0:T(8,128)(2,1)}) custom-call(bf16[3,256,2048]{2,1,0:T(8,128)(2,1)} %bitcast.24, bf16[512,3072]{1,0:T(8,128)(2,1)} %rows.1), custom_call_target="tpu_custom_call" | custom-call | bytes 300000000 | tf_op jit(solution)/shard_map/pallas_call | solution.py:104
  167.3 0.0 copy-start.5
  167.3 1.7 copy.12
  169.0 1.6 copy.13
  170.6 14.9 %all-reduce.2.cloned.1.call-done = bf16[256,4096]{1,0:T(8,128)(2,1)} async-done(((bf16[256,4096]{1,0:T(8,128)(2,1)}), bf16[256,4096]{1,0:T(8,128)(2,1)}) %all-reduce.2.cloned.1.call-update) | async-done | bytes 2097168 | tf_op jit(solution)/shard_map/psum | solution.py:309
  185.5 2.1 fusion.2
  187.6 0.0 copy-done.5
  187.6 0.0 copy-start.1
  187.6 6.5 %fusion.15.text_k.text_v = bf16[2,256,512]{2,1,0:T(8,128)(2,1)S(1)} fusion(bf16[4096,2,512]{2,1,0:T(2,128)(2,1)} %param.12, bf16[256,4096]{1,0:T(8,128)(2,1)} %all-reduce.2.cloned.1.call-done, f32[4096]{0:T(1024)S(1)} %copy-done.5, f32[256]{0:T(256)S(1)} %add_rsqrt_fusion), kind=kOutput, calls=%fused_computation.14 | convolution fusion | flops 2151940096 | bytes 11027456 | tf_op jit(solution)/shard_map/td,dkh->kth/dot_general | solution.py:315
  194.2 14.8 %shard_map.96.attn = bf16[1024,512]{1,0:T(8,128)(2,1)S(1)} custom-call(s32[1]{0:T(128)S(6)} %copy.21.length, bf16[3,1024,512]{2,1,0:T(8,128)(2,1)S(1)} %copy-done.1, bf16[3,1024,512]{2,1,0:T(8,128)(2,1)S(1)} %copy-done.1, bf16[3,1024,512]{2,1,0:T(8,128)(2,1)S(1)} %copy-done.1, bf16[2,256,512]{2,1,0:T(8,128)(2,1)S(1)} %fusion.15.text_k.text_v, ...), custom_call_target="tpu_custom_call" | custom-call | tf_op jit(solution)/shard_map/pallas_call | solution.py:191
  209.0 1.0 copy-done.2
  210.1 31.4 %shard_map.97.attn = bf16[256,2048]{1,0:T(8,128)(2,1)} custom-call(bf16[1024,512]{1,0:T(8,128)(2,1)} %copy-done.2), custom_call_target="tpu_custom_call" | custom-call | bytes 60000000 | tf_op jit(solution)/shard_map/pallas_call | solution.py:155
  241.5 1.2 copy-done.3
  242.7 81.3 %shard_map.98 = bf16[2048,384]{1,0:T(8,128)(2,1)} custom-call(bf16[256,2048]{1,0:T(8,128)(2,1)S(1)} %copy-done.3, bf16[8,256,384]{2,1,0:T(8,128)(2,1)} %bitcast.23), custom_call_target="tpu_custom_call" | custom-call | bytes 200000000 | tf_op jit(solution)/shard_map/pallas_call | solution.py:282
  324.0 0.0 reduce-scatter.2.cloned.1.call-update
  324.1 9.1 %fusion.5 = bf16[1,256,3072]{2,1,0:T(8,128)(2,1)} fusion(bf16[256,2048]{1,0:T(8,128)(2,1)S(1)} %copy-done.4, bf16[2048,3072]{1,0:T(8,128)(2,1)} %get-tuple-element.12), kind=kOutput, calls=%fused_computation.9 | convolution fusion | flops 3222011904 | bytes 15204352 | tf_op jit(solution)/shard_map/dot_general | solution.py:323
  333.1 31.4 %reduce-scatter.2.cloned.1.call-done = bf16[512,384]{1,0:T(8,128)(2,1)} async-done(((bf16[2048,384]{1,0:T(8,128)(2,1)}), bf16[512,384]{1,0:T(8,128)(2,1)}) %reduce-scatter.2.cloned.1.call-update) | async-done | bytes 393232 | tf_op jit(solution)/shard_map/reduce_scatter | solution.py:320
  364.6 1.9 convert_element_type.26
  (6 shorter events, 0.0 us)
Async XLA Ops:
  7.2 1.1 copy-start
  7.2 178.3 %all-reduce.2.cloned.1.call-start = ((), (), s32[]{:S(2)}) async-start(), calls=%async_computation.1 | async-start | bytes 4194304 | tf_op jit(solution)/shard_map/psum | solution.py:309
  16.3 348.2 %reduce-scatter.2.cloned.1.call-start = ((), (), s32[]{:S(2)}) async-start(), calls=%async_computation.2 | async-start | bytes 1966080 | tf_op jit(solution)/shard_map/reduce_scatter | solution.py:320
  167.3 20.3 %copy-start.5 = (f32[4096]{0:T(1024)S(1)}, f32[4096]{0:T(1024)}, u32[]{:S(2)}) copy-start(f32[4096]{0:T(1024)} %param.10) | copy-start | bytes 49156
  187.6 6.6 %copy-start.1 = (bf16[3,1024,512]{2,1,0:T(8,128)(2,1)S(1)}, bf16[3,1024,512]{2,1,0:T(8,128)(2,1)}, u32[]{:S(2)}) copy-start(bf16[3,1024,512]{2,1,0:T(8,128)(2,1)} %get-tuple-element.10.q.k.v) | copy-start | bytes 9437188
  209.0 1.0 copy-start.2
  241.5 1.2 copy-start.3
  242.7 81.3 %copy-start.4 = (bf16[256,2048]{1,0:T(8,128)(2,1)S(1)}, bf16[256,2048]{1,0:T(8,128)(2,1)}, u32[]{:S(2)}) copy-start(bf16[256,2048]{1,0:T(8,128)(2,1)} %shard_map.97.attn) | copy-start | bytes 3145732
Sparse Core Ops, SparseCore 0:
  16.5 169.0 all-reduce.1
  324.2 40.3 reduce-scatter.1

commit v4 on v3

--- a/solution.py
+++ b/solution.py
@@ -203,33 +203,37 @@
 
 
 def gradient_kernel(
-    chips, attn, cotangent, out, turned, give, got, keep, land, g_s, g_r, k_s, k_r
+    n, chips, attn, cotangent, out, turned, give, got, keep, land, part, come,
+    g_s, g_r, k_s, k_r, s_s, s_r
 ):
     me, dp = lax.axis_index("seq"), lax.axis_index("dp")
     chip, core = dp // 2, dp % 2
     other = 2 * chip + 1 - core
-    wide = out.shape[0]
-    tile = math.gcd(wide, 512)
+    wide, block = attn.shape[1], out.shape[0]
+    tile = math.gcd(block, 512)
 
     barrier = pltpu.get_barrier_semaphore()
     for k in range(1, chips):
         to = 2 * lax.rem(chip + k, chips) + core
         pl.semaphore_signal(barrier, inc=1, device_id=(to, me), device_id_type=MESH)
     pl.semaphore_signal(barrier, inc=1, device_id=(other, me), device_id_type=MESH)
+    for r in range(1, n):
+        to = lax.rem(me + r, n)
+        pl.semaphore_signal(barrier, inc=1, device_id=(dp, to), device_id_type=MESH)
     turned[...] = attn[...].T
-    pl.semaphore_wait(barrier, chips)
+    pl.semaphore_wait(barrier, chips + n - 1)
 
     def remote(src, dst, send, recv, to):
         return pltpu.make_async_remote_copy(
             src_ref=src, dst_ref=dst, send_sem=send, recv_sem=recv, device_id=to, device_id_type=MESH
         )
 
-    def tiles(body):
+    def tiles(body, first, count):
         def step(t, carry):
-            body(pl.ds(pl.multiple_of(t * tile, tile), tile))
+            body(pl.ds(pl.multiple_of(first + t * tile, tile), tile))
             return carry
 
-        lax.fori_loop(0, wide // tile, step, 0)
+        lax.fori_loop(0, count // tile, step, 0)
 
     def term(rows, index):
         return jnp.dot(turned[rows, :], cotangent[index], preferred_element_type=jnp.float32)
@@ -242,37 +246,61 @@
         def fill(rows):
             give[k, rows, :] = term(rows, index).astype(give.dtype)
 
-        tiles(fill)
+        tiles(fill, 0, wide)
         gives[k] = remote(give.at[k], got.at[k], g_s.at[k], g_r.at[k], (other, me))
         gives[k].start()
-    for k in range(1, chips):
-        index = 2 * lax.rem(chip + k, chips) + core
-        gives[k].wait_recv()
-
-        def add(rows):
-            both = term(rows, index) + got[k, rows, :].astype(jnp.float32)
-            keep[k - 1, rows, :] = both.astype(keep.dtype)
-
-        tiles(add)
-        keeps.append(remote(keep.at[k - 1], land.at[k - 1], k_s.at[k - 1], k_r.at[k - 1], (index, me)))
-        keeps[-1].start()
+    turns = list(range(1, n)) + [0]
+    for r in turns:
+        first = pl.multiple_of(lax.rem(me + r, n) * block, block)
+        rows_of = pl.ds(first, block)
+        for k in range(1, chips):
+            index = 2 * lax.rem(chip + k, chips) + core
+            if r == turns[0]:
+                gives[k].wait_recv()
+
+            def add(rows):
+                both = term(rows, index) + got[k, rows, :].astype(jnp.float32)
+                keep[k - 1, rows, :] = both.astype(keep.dtype)
+
+            tiles(add, first, block)
+            keeps.append(
+                remote(
+                    keep.at[k - 1, rows_of], land.at[k - 1, rows_of],
+                    k_s.at[k - 1, r], k_r.at[k - 1, r], (index, me),
+                )
+            )
+            keeps[-1].start()
     gives[0].wait_recv()
-    for copy in keeps:
-        copy.wait_recv()
-
-    def finish(rows):
-        total = term(rows, dp) + got[0, rows, :].astype(jnp.float32)
+
+    def total(rows):
+        value = term(rows, dp) + got[0, rows, :].astype(jnp.float32)
         for k in range(1, chips):
-            total += land[k - 1, rows, :].astype(jnp.float32)
-        out[rows, :] = total.astype(out.dtype)
-
-    tiles(finish)
-    for copy in list(gives.values()) + keeps:
+            value += land[k - 1, rows, :].astype(jnp.float32)
+        return value
+
+    sends = []
+    for turn, r in enumerate(turns):
+        to = lax.rem(me + r, n)
+        rows = pl.ds(pl.multiple_of(to * block, block), block)
+        for k in range(1, chips):
+            keeps[turn * (chips - 1) + k - 1].wait_recv()
+        if r:
+            part[r - 1] = total(rows).astype(part.dtype)
+            sends.append(remote(part.at[r - 1], come.at[r - 1], s_s.at[r - 1], s_r.at[r - 1], (dp, to)))
+            sends[-1].start()
+        else:
+            value = total(rows)
+            for copy in sends:
+                copy.wait_recv()
+            for k in range(1, n):
+                value += come[k - 1].astype(jnp.float32)
+            out[...] = value
+    for copy in list(gives.values()) + keeps + sends:
         copy.wait_send()
 
 
 def gradient(attn, cotangent):
-    parts = lax.axis_size("dp")
+    n, parts = lax.axis_size("seq"), lax.axis_size("dp")
     chips = parts // 2
     tokens, wide = attn.shape
     width = cotangent.shape[1] // parts
@@ -280,17 +308,20 @@
     vmem = pl.BlockSpec(memory_space=pltpu.VMEM)
     dma = pltpu.SemaphoreType.DMA
     return pl.pallas_call(
-        functools.partial(gradient_kernel, chips),
+        functools.partial(gradient_kernel, n, chips),
         in_specs=[vmem, vmem],
         out_specs=vmem,
-        out_shape=jax.ShapeDtypeStruct((wide, width), jnp.bfloat16),
+        out_shape=jax.ShapeDtypeStruct((wide // n, width), jnp.float32),
         scratch_shapes=[
             pltpu.VMEM((wide, tokens), jnp.bfloat16),
             pltpu.VMEM((chips, wide, width), jnp.bfloat16),
             pltpu.VMEM((chips, wide, width), jnp.bfloat16),
             pltpu.VMEM((chips - 1, wide, width), jnp.bfloat16),
             pltpu.VMEM((chips - 1, wide, width), jnp.bfloat16),
-            dma((chips,)), dma((chips,)), dma((chips - 1,)), dma((chips - 1,)),
+            pltpu.VMEM((n - 1, wide // n, width), jnp.bfloat16),
+            pltpu.VMEM((n - 1, wide // n, width), jnp.bfloat16),
+            dma((chips,)), dma((chips,)), dma((chips - 1, n)), dma((chips - 1, n)),
+            dma((n - 1,)), dma((n - 1,)),
         ],
         compiler_params=pltpu.CompilerParams(
             collective_id=2, has_side_effects=True, vmem_limit_bytes=52 * 2**20
@@ -316,10 +347,7 @@
         "td,dkh->kth", text_emb, text_kv, preferred_element_type=jnp.float32
     ).astype(jnp.bfloat16)
     rows = give_back(attend(heads, text, text_len))
-    columns = gradient(rows, output_cotangent[0])
-    output_weight_gradient = lax.psum_scatter(
-        columns, "seq", scatter_dimension=0, tiled=True
-    ).astype(jnp.float32)
+    output_weight_gradient = gradient(rows, output_cotangent[0])
     projected = jnp.dot(rows, weight, preferred_element_type=jnp.float32)
     return (projected.astype(jnp.bfloat16)[None], output_weight_gradient)
 

time: 374 us -> 343 us (0.917)
  waiting for transfers between devices: 46.4 us -> 14.9 us
    reduce_scatter x1 -> x0, waiting for transfers between devices: 31.4 us -> none  [shards(): lax.psum_scatter(columns, 'seq', scatter_dimension=0, tiled=True)]
  transfers between devices with their start and end apart: 2 -> 1, of which waited for: 2 -> 1; matrix products, arithmetic and copies ran while one was open for 3% -> 1% of each run, Pallas kernels for 40% -> 44%
where the time goes in v4:
time: 343 us
  Pallas kernels  281 us (82%)
  matrix products  24.1 us (7%)
  waiting for transfers between devices  14.9 us (4%)
  between operations  14.8 us (4%)
  local copies, waits for them, and re-layouts  6.19 us (2%)
    pallas_call x1, Pallas kernels, collect(): pl.pallas_call(functools.partial(collect_kernel, n, chips), out_shape=(ja...  150 us
    pallas_call x1, Pallas kernels, gradient(): pl.pallas_call(functools.partial(gradient_kernel, n, chips), in_specs=[vm...  84.3 us
    pallas_call x1, Pallas kernels, give_back(): pl.pallas_call(functools.partial(return_kernel, n), out_shape=jax.ShapeDt...  31.5 us
    psum x1, waiting for transfers between devices, shards(): summed = lax.psum(partial_value, 'seq')  14.9 us
    pallas_call x1, Pallas kernels, attend(): pl.pallas_call(attend_kernel, grid=(width // HD, latent // rows), in_spec...  14.8 us
    dot_general x1, matrix products, shards(): projected = jnp.dot(rows, weight, preferred_element_type=jnp.float32)  9.54 us
    dot_general x1, matrix products, shards(): jnp.dot(enc_hidden[0], enc_wo, preferred_element_type=jnp.float32)  8.06 us
  transfers between devices with their start and end apart: 1, of which 1 were waited for; matrix products, arithmetic and copies ran while one was open for 1% of the time, Pallas kernels for 44%

profile of v4, /device:TPU:0, one launch (start us, length us, event | category | flops | bytes accessed | tf_op | source)
XLA Modules:
  0.0 343.0 jit_solution(9384205397669200963)
XLA Ops:
  7.2 0.0 copy-start
  7.2 0.0 all-reduce.2.cloned.1.call-start
  7.2 1.0 copy-done
  8.3 8.1 %convolution_convert_fusion = bf16[256,4096]{1,0:T(8,128)(2,1)} fusion(bf16[1280,4096]{1,0:T(8,128)(2,1)} %param.9, bf16[1,256,1280]{2,1,0:T(8,128)(2,1)S(1)} %copy-done), kind=kOutput, calls=%fused_computation.4 | convolution fusion | flops 2685403136 | bytes 13238272 | tf_op jit(solution)/shard_map/dot_general | solution.py:336
  16.3 0.0 all-reduce.2.cloned.1.call-update
  17.0 150.2 %shard_map.95 = (bf16[3,1024,512]{2,1,0:T(8,128)(2,1)}, bf16[2048,3072]{1,0:T(8,128)(2,1)}) custom-call(bf16[3,256,2048]{2,1,0:T(8,128)(2,1)} %bitcast.24, bf16[512,3072]{1,0:T(8,128)(2,1)} %rows.1), custom_call_target="tpu_custom_call" | custom-call | bytes 300000000 | tf_op jit(solution)/shard_map/pallas_call | solution.py:104
  167.2 0.0 copy-start.4
  167.3 1.7 copy.12
  169.0 1.6 copy.13
  170.6 14.9 %all-reduce.2.cloned.1.call-done = bf16[256,4096]{1,0:T(8,128)(2,1)} async-done(((bf16[256,4096]{1,0:T(8,128)(2,1)}), bf16[256,4096]{1,0:T(8,128)(2,1)}) %all-reduce.2.cloned.1.call-update) | async-done | bytes 2097168 | tf_op jit(solution)/shard_map/psum | solution.py:340
  185.5 2.1 fusion.2
  187.6 0.0 copy-done.4
  187.6 0.0 copy-start.1
  187.6 6.5 %fusion.15.text_k.text_v = bf16[2,256,512]{2,1,0:T(8,128)(2,1)S(1)} fusion(bf16[4096,2,512]{2,1,0:T(2,128)(2,1)} %param.12, bf16[256,4096]{1,0:T(8,128)(2,1)} %all-reduce.2.cloned.1.call-done, f32[4096]{0:T(1024)S(1)} %copy-done.4, f32[256]{0:T(256)S(1)} %add_rsqrt_fusion), kind=kOutput, calls=%fused_computation.14 | convolution fusion | flops 2151940096 | bytes 11027456 | tf_op jit(solution)/shard_map/td,dkh->kth/dot_general | solution.py:346
  194.1 0.0 copy-done.1
  194.1 14.8 %shard_map.96.attn = bf16[1024,512]{1,0:T(8,128)(2,1)S(1)} custom-call(s32[1]{0:T(128)S(6)} %copy.22.length, bf16[3,1024,512]{2,1,0:T(8,128)(2,1)S(1)} %copy-done.1, bf16[3,1024,512]{2,1,0:T(8,128)(2,1)S(1)} %copy-done.1, bf16[3,1024,512]{2,1,0:T(8,128)(2,1)S(1)} %copy-done.1, bf16[2,256,512]{2,1,0:T(8,128)(2,1)S(1)} %fusion.15.text_k.text_v, ...), custom_call_target="tpu_custom_call" | custom-call | tf_op jit(solution)/shard_map/pallas_call | solution.py:191
  209.0 0.0 copy-start.2
  209.0 1.0 copy-done.2
  209.9 31.5 %shard_map.97.attn = bf16[256,2048]{1,0:T(8,128)(2,1)} custom-call(bf16[1024,512]{1,0:T(8,128)(2,1)} %copy-done.2), custom_call_target="tpu_custom_call" | custom-call | bytes 60000000 | tf_op jit(solution)/shard_map/pallas_call | solution.py:155
  241.4 0.0 copy-start.3
  241.4 9.5 %fusion.5 = bf16[1,256,3072]{2,1,0:T(8,128)(2,1)} fusion(bf16[256,2048]{1,0:T(8,128)(2,1)} %shard_map.97.attn, bf16[2048,3072]{1,0:T(8,128)(2,1)} %get-tuple-element.12), kind=kOutput, calls=%fused_computation.9 | convolution fusion | flops 3222011904 | bytes 15204352 | tf_op jit(solution)/shard_map/dot_general | solution.py:351
  251.0 0.0 copy-done.3
  251.0 84.3 %shard_map.98 = f32[512,384]{1,0:T(8,128)S(1)} custom-call(bf16[256,2048]{1,0:T(8,128)(2,1)S(1)} %copy-done.3, bf16[8,256,384]{2,1,0:T(8,128)(2,1)} %bitcast.23), custom_call_target="tpu_custom_call" | custom-call | bytes 200000000 | tf_op jit(solution)/shard_map/pallas_call | solution.py:310
  335.3 0.9 copy.23
  (1 shorter events, 0.0 us)
Async XLA Ops:
  7.2 1.1 copy-start
  7.2 178.3 %all-reduce.2.cloned.1.call-start = ((), (), s32[]{:S(2)}) async-start(), calls=%async_computation | async-start | bytes 4194304 | tf_op jit(solution)/shard_map/psum | solution.py:340
  167.2 20.3 %copy-start.4 = (f32[4096]{0:T(1024)S(1)}, f32[4096]{0:T(1024)}, u32[]{:S(2)}) copy-start(f32[4096]{0:T(1024)} %param.10) | copy-start | bytes 49156
  187.6 6.6 %copy-start.1 = (bf16[3,1024,512]{2,1,0:T(8,128)(2,1)S(1)}, bf16[3,1024,512]{2,1,0:T(8,128)(2,1)}, u32[]{:S(2)}) copy-start(bf16[3,1024,512]{2,1,0:T(8,128)(2,1)} %get-tuple-element.10.q.k.v) | copy-start | bytes 9437188
  209.0 1.0 copy-start.2
  241.4 9.5 %copy-start.3 = (bf16[256,2048]{1,0:T(8,128)(2,1)S(1)}, bf16[256,2048]{1,0:T(8,128)(2,1)}, u32[]{:S(2)}) copy-start(bf16[256,2048]{1,0:T(8,128)(2,1)} %shard_map.97.attn) | copy-start | bytes 3145732
Sparse Core Ops, SparseCore 0:
  16.5 168.9 all-reduce.1

commit v5 on v4

--- a/solution.py
+++ b/solution.py
@@ -203,7 +203,8 @@
 
 
 def gradient_kernel(
-    n, chips, attn, cotangent, out, turned, give, got, keep, land, part, come,
+    n, chips, attn, cotangent, weight, out, projected, turned, give, got, keep, land, part, come,
+    held, w_s,
     g_s, g_r, k_s, k_r, s_s, s_r
 ):
     me, dp = lax.axis_index("seq"), lax.axis_index("dp")
@@ -220,6 +221,8 @@
     for r in range(1, n):
         to = lax.rem(me + r, n)
         pl.semaphore_signal(barrier, inc=1, device_id=(dp, to), device_id_type=MESH)
+    bring = pltpu.make_async_copy(weight, held, w_s)
+    bring.start()
     turned[...] = attn[...].T
     pl.semaphore_wait(barrier, chips + n - 1)
 
@@ -270,6 +273,17 @@
                 )
             )
             keeps[-1].start()
+    bring.wait()
+    step_width = math.gcd(projected.shape[1], 512)
+
+    def project(t, carry):
+        cols = pl.ds(pl.multiple_of(t * step_width, step_width), step_width)
+        projected[:, cols] = jnp.dot(
+            attn[...], held[:, cols], preferred_element_type=jnp.float32
+        ).astype(projected.dtype)
+        return carry
+
+    lax.fori_loop(0, projected.shape[1] // step_width, project, 0)
     gives[0].wait_recv()
 
     def total(rows):
@@ -299,7 +313,7 @@
         copy.wait_send()
 
 
-def gradient(attn, cotangent):
+def gradient(attn, cotangent, weight):
     n, parts = lax.axis_size("seq"), lax.axis_size("dp")
     chips = parts // 2
     tokens, wide = attn.shape
@@ -309,9 +323,12 @@
     dma = pltpu.SemaphoreType.DMA
     return pl.pallas_call(
         functools.partial(gradient_kernel, n, chips),
-        in_specs=[vmem, vmem],
-        out_specs=vmem,
-        out_shape=jax.ShapeDtypeStruct((wide // n, width), jnp.float32),
+        in_specs=[vmem, vmem, ANY],
+        out_specs=(vmem, vmem),
+        out_shape=(
+            jax.ShapeDtypeStruct((wide // n, width), jnp.float32),
+            jax.ShapeDtypeStruct((tokens, weight.shape[1]), jnp.bfloat16),
+        ),
         scratch_shapes=[
             pltpu.VMEM((wide, tokens), jnp.bfloat16),
             pltpu.VMEM((chips, wide, width), jnp.bfloat16),
@@ -320,14 +337,16 @@
             pltpu.VMEM((chips - 1, wide, width), jnp.bfloat16),
             pltpu.VMEM((n - 1, wide // n, width), jnp.bfloat16),
             pltpu.VMEM((n - 1, wide // n, width), jnp.bfloat16),
+            pltpu.VMEM(weight.shape, jnp.bfloat16),
+            dma,
             dma((chips,)), dma((chips,)), dma((chips - 1, n)), dma((chips - 1, n)),
             dma((n - 1,)), dma((n - 1,)),
         ],
         compiler_params=pltpu.CompilerParams(
-            collective_id=2, has_side_effects=True, vmem_limit_bytes=52 * 2**20
+            collective_id=2, has_side_effects=True, vmem_limit_bytes=58 * 2**20
         ),
         cost_estimate=pl.CostEstimate(flops=0, bytes_accessed=200_000_000, transcendentals=0),
-    )(attn, cotangent)
+    )(attn, cotangent, weight)
 
 
 def shards(
@@ -347,9 +366,8 @@
         "td,dkh->kth", text_emb, text_kv, preferred_element_type=jnp.float32
     ).astype(jnp.bfloat16)
     rows = give_back(attend(heads, text, text_len))
-    output_weight_gradient = gradient(rows, output_cotangent[0])
-    projected = jnp.dot(rows, weight, preferred_element_type=jnp.float32)
-    return (projected.astype(jnp.bfloat16)[None], output_weight_gradient)
+    output_weight_gradient, projected = gradient(rows, output_cotangent[0], weight)
+    return (projected[None], output_weight_gradient)
 
 
 def solution(mesh):

time: 343 us -> 340 us (level)
  matrix products: 24.1 us -> 14.6 us
  local copies, waits for them, and re-layouts: 6.19 us -> 10.1 us
    dot_general x1 -> x0, matrix products: 9.54 us -> none  [shards(): projected = jnp.dot(rows, weight, preferred_element_type=jnp.float32)]
    unnamed x11 -> x10, local copies, waits for them, and re-layouts: 2.9 us -> 6.79 us
where the time goes in v5:
time: 340 us; the launch traced here: 339 us
  Pallas kernels  283 us (83%)
  waiting for transfers between devices  14.9 us (4%)
  between operations  14.8 us (4%)
  matrix products  14.6 us (4%)
  local copies, waits for them, and re-layouts  10.1 us (3%)
    pallas_call x1, Pallas kernels, collect(): pl.pallas_call(functools.partial(collect_kernel, n, chips), out_shape=(ja...  150 us
    pallas_call x1, Pallas kernels, gradient(): pl.pallas_call(functools.partial(gradient_kernel, n, chips), in_specs=[vm...  86.1 us
    pallas_call x1, Pallas kernels, give_back(): pl.pallas_call(functools.partial(return_kernel, n), out_shape=jax.ShapeDt...  31.5 us
    psum x1, waiting for transfers between devices, shards(): summed = lax.psum(partial_value, 'seq')  14.9 us
    pallas_call x1, Pallas kernels, attend(): pl.pallas_call(attend_kernel, grid=(width // HD, latent // rows), in_spec...  14.8 us
    dot_general x1, matrix products, shards(): jnp.dot(enc_hidden[0], enc_wo, preferred_element_type=jnp.float32)  8.06 us
  transfers between devices with their start and end apart: 1, of which 1 were waited for; matrix products, arithmetic and copies ran while one was open for 1% of the time, Pallas kernels for 44%

profile of v5, /device:TPU:0, one launch (start us, length us, event | category | flops | bytes accessed | tf_op | source)
XLA Modules:
  0.0 339.2 jit_solution(13634682328845328455)
XLA Ops:
  7.2 0.0 copy-start
  7.2 0.0 all-reduce.2.cloned.1.call-start
  7.2 1.0 copy-done
  8.3 8.1 %convolution_convert_fusion = bf16[256,4096]{1,0:T(8,128)(2,1)} fusion(bf16[1280,4096]{1,0:T(8,128)(2,1)} %param.9, bf16[1,256,1280]{2,1,0:T(8,128)(2,1)S(1)} %copy-done), kind=kOutput, calls=%fused_computation.4 | convolution fusion | flops 2685403136 | bytes 13238272 | tf_op jit(solution)/shard_map/dot_general | solution.py:355
  16.3 0.0 all-reduce.2.cloned.1.call-update
  17.0 150.2 %shard_map.95 = (bf16[3,1024,512]{2,1,0:T(8,128)(2,1)}, bf16[2048,3072]{1,0:T(8,128)(2,1)}) custom-call(bf16[3,256,2048]{2,1,0:T(8,128)(2,1)} %bitcast.21, bf16[512,3072]{1,0:T(8,128)(2,1)} %rows.1), custom_call_target="tpu_custom_call" | custom-call | bytes 300000000 | tf_op jit(solution)/shard_map/pallas_call | solution.py:104
  167.2 0.0 copy-start.3
  167.2 1.7 copy.12
  169.0 1.6 copy.13
  170.5 14.9 %all-reduce.2.cloned.1.call-done = bf16[256,4096]{1,0:T(8,128)(2,1)} async-done(((bf16[256,4096]{1,0:T(8,128)(2,1)}), bf16[256,4096]{1,0:T(8,128)(2,1)}) %all-reduce.2.cloned.1.call-update) | async-done | bytes 2097168 | tf_op jit(solution)/shard_map/psum | solution.py:359
  185.5 2.1 fusion.2
  187.6 0.0 copy-done.3
  187.6 0.0 copy-start.1
  187.6 6.5 %fusion.14.text_k.text_v = bf16[2,256,512]{2,1,0:T(8,128)(2,1)S(1)} fusion(bf16[4096,2,512]{2,1,0:T(2,128)(2,1)} %param.12, bf16[256,4096]{1,0:T(8,128)(2,1)} %all-reduce.2.cloned.1.call-done, f32[4096]{0:T(1024)S(1)} %copy-done.3, f32[256]{0:T(256)S(1)} %add_rsqrt_fusion), kind=kOutput, calls=%fused_computation.12 | convolution fusion | flops 2151940096 | bytes 11027456 | tf_op jit(solution)/shard_map/td,dkh->kth/dot_general | solution.py:365
  194.1 0.0 copy-done.1
  194.1 14.8 %shard_map.96.attn = bf16[1024,512]{1,0:T(8,128)(2,1)S(1)} custom-call(s32[1]{0:T(128)S(6)} %copy.23.length, bf16[3,1024,512]{2,1,0:T(8,128)(2,1)S(1)} %copy-done.1, bf16[3,1024,512]{2,1,0:T(8,128)(2,1)S(1)} %copy-done.1, bf16[3,1024,512]{2,1,0:T(8,128)(2,1)S(1)} %copy-done.1, bf16[2,256,512]{2,1,0:T(8,128)(2,1)S(1)} %fusion.14.text_k.text_v, ...), custom_call_target="tpu_custom_call" | custom-call | tf_op jit(solution)/shard_map/pallas_call | solution.py:191
  209.0 0.0 copy-start.2
  209.0 1.0 copy-done.2
  210.0 31.5 %shard_map.97.attn = bf16[256,2048]{1,0:T(8,128)(2,1)} custom-call(bf16[1024,512]{1,0:T(8,128)(2,1)} %copy-done.2), custom_call_target="tpu_custom_call" | custom-call | bytes 60000000 | tf_op jit(solution)/shard_map/pallas_call | solution.py:155
  241.5 86.1 %shard_map.98 = (f32[512,384]{1,0:T(8,128)}, bf16[256,3072]{1,0:T(8,128)(2,1)}) custom-call(bf16[256,2048]{1,0:T(8,128)(2,1)} %shard_map.97.attn, bf16[8,256,384]{2,1,0:T(8,128)(2,1)} %bitcast.19, bf16[2048,3072]{1,0:T(8,128)(2,1)} %get-tuple-element.15.weight), custom_call_target="tpu_custom_call" | custom-call | bytes 200000000 | tf_op jit(solution)/shard_map/pallas_call | solution.py:324
  327.6 2.7 copy.24
  330.3 2.1 copy.25
  (1 shorter events, 0.0 us)
Async XLA Ops:
  7.2 1.1 copy-start
  7.2 178.3 %all-reduce.2.cloned.1.call-start = ((), (), s32[]{:S(2)}) async-start(), calls=%async_computation | async-start | bytes 4194304 | tf_op jit(solution)/shard_map/psum | solution.py:359
  167.2 20.3 %copy-start.3 = (f32[4096]{0:T(1024)S(1)}, f32[4096]{0:T(1024)}, u32[]{:S(2)}) copy-start(f32[4096]{0:T(1024)} %param.10) | copy-start | bytes 49156
  187.6 6.6 %copy-start.1 = (bf16[3,1024,512]{2,1,0:T(8,128)(2,1)S(1)}, bf16[3,1024,512]{2,1,0:T(8,128)(2,1)}, u32[]{:S(2)}) copy-start(bf16[3,1024,512]{2,1,0:T(8,128)(2,1)} %get-tuple-element.12.q.k.v) | copy-start | bytes 9437188
  209.0 1.0 copy-start.2
Sparse Core Ops, SparseCore 0:
  16.5 168.9 all-reduce.1
